TPU v7x, 32 devices: a whole 2x2x4 slice. The times are simulated.
32 devices in a mesh: section: 2 (over core), dev: 16 (over z, y, x).
Axes of the slice: x: 2, y: 2, z: 4, core: 2. Of those that a mesh axis runs over, the one named last changes fastest.
Arguments:
- token_ids: int32 [1, 16], replicated, may hold values from 0 to 32127
- slot_of: int32 [16], replicated, may hold values from 0 to 15, each once
- lengths: int32 [16], replicated, may hold values from 257 to 1024, as said below
- block_table: int32 [16, 8], replicated, may hold values from 0 to 127, as said below
- kv_pool: bfloat16 [2, 128, 128, 2048], P(None, None, 'dev', 'section'), may hold values from -30 to 30
- self_cache: bfloat16 [2, 16, 128, 2048], P(None, 'dev', None, 'section'), may hold values from -30 to 30
- embedding: bfloat16 [32128, 4096], P(None, 'dev'), may hold values from -30 to 30
- norm_self: float32 [4096], P('dev'), may hold values from 0.25 to 1.75
- norm_cross: float32 [4096], P('dev'), may hold values from 0.25 to 1.75
- norm_ffn: float32 [4096], P('dev'), may hold values from 0.25 to 1.75
- w_self_qkv: bfloat16 [4096, 3, 2048], P('dev', None, 'section'), may hold values from -0.09375 to 0.09375
- w_self_out: bfloat16 [2048, 4096], P('section', 'dev'), may hold values from -0.125 to 0.125
- w_cross_q: bfloat16 [4096, 2048], P('dev', 'section'), may hold values from -0.09375 to 0.09375
- w_cross_out: bfloat16 [2048, 4096], P('section', 'dev'), may hold values from -0.125 to 0.125
- w_in: bfloat16 [4096, 2, 5120], P('dev', None, 'section'), may hold values from -0.09375 to 0.09375
- w_out: bfloat16 [5120, 4096], P('section', 'dev'), may hold values from -0.078125 to 0.078125
Outputs:
- out: bfloat16 [1, 16, 4096], P(None, None, 'dev')
Inputs may be any that keep to these rules, and one draw needn't show every extreme that they name: A permutation: request r occupies decoder slot slot_of[r]. `lengths`: one request has exactly 1024 source tokens. `block_table`: all entries differ.
All inputs are finite; a program needn't handle non-finite values.
Results may differ from a plain program's by a relative error of at most 0.008.
Values may be sent and summed in bfloat16 or wider, within the bound.
A program may use at most 128 MiB of HBM per device.

v0:
```python
import jax
import jax.numpy as jnp
from jax import lax
from jax.sharding import PartitionSpec as P

DH = 64
MAXB = 8
STEPS = 1


EPS = 1e-06


def rms_norm(resid, gain, width):
    total = lax.psum(jnp.sum(resid * resid, axis=1), "dev")
    scale = lax.rsqrt(total / width + EPS)
    return (resid * scale[:, None] * gain[None, :]).astype(jnp.bfloat16)


def to_owner(normed, weight):
    flat = weight.reshape(weight.shape[0], -1)
    return lax.psum_scatter(
        jnp.dot(normed, flat, preferred_element_type=jnp.float32),
        "dev",
        scatter_dimension=0,
        tiled=True,
    )


def from_owner(active, weight):
    partial_rows = jnp.dot(
        lax.all_gather(active, "dev", axis=0, tiled=True),
        weight,
        preferred_element_type=jnp.float32,
    )
    return lax.psum(partial_rows, "section")


def attend(query, keys, values, valid):
    scores = jnp.einsum("rhe,rjhe->rhj", query, keys, preferred_element_type=jnp.float32)
    mask = valid[:, None, :]
    top = jnp.max(jnp.where(mask, scores, -jnp.inf), axis=2, keepdims=True)
    weights = jnp.where(mask, jnp.exp(jnp.where(mask, scores, top) - top), 0.0)
    total = jnp.sum(weights, axis=2)
    mixed = jnp.einsum(
        "rhj,rjhe->rhe", weights.astype(jnp.bfloat16), values, preferred_element_type=jnp.float32
    )
    return (mixed / total[:, :, None]).astype(jnp.bfloat16)


def local(
    token_ids,
    slot_of,
    lengths,
    block_table,
    kv_pool,
    self_cache,
    embedding,
    norm_self,
    norm_cross,
    norm_ffn,
    w_self_qkv,
    w_self_out,
    w_cross_q,
    w_cross_out,
    w_in,
    w_out,
):
    dev_count = lax.axis_size("dev")
    requests = slot_of.shape[0]
    own = requests // dev_count
    width = embedding.shape[1] * dev_count
    half_inner = w_cross_q.shape[1]
    heads_here = half_inner // DH
    here = lax.axis_index("dev")
    order = jnp.argsort(slot_of)
    len_slot = lengths[order]
    own_len = lax.dynamic_slice_in_dim(len_slot, here * own, own, 0)
    table_slot = block_table[order]
    ids_slot = token_ids[:, order]
    rows_here = kv_pool.shape[2]
    span = MAXB * rows_here * dev_count
    picked = kv_pool[:, table_slot.reshape(-1)]
    arrived = lax.all_to_all(picked, "dev", split_axis=1, concat_axis=2, tiled=True)
    src_keys = arrived[0].reshape(own, span, heads_here, DH)
    src_values = arrived[1].reshape(own, span, heads_here, DH)
    valid_rows = jnp.arange(span)[None, :] < own_len[:, None]
    cache_keys = self_cache[0]
    cache_values = self_cache[1]
    prev = cache_keys.shape[1]
    count = prev + STEPS
    new_keys = jnp.zeros((own, STEPS, half_inner), jnp.bfloat16)
    new_values = jnp.zeros((own, STEPS, half_inner), jnp.bfloat16)
    resid = embedding[ids_slot[0]].astype(jnp.float32)
    normed = rms_norm(resid, norm_self, width)
    qkv = to_owner(normed, w_self_qkv).astype(jnp.bfloat16).reshape(own, 3, half_inner)
    new_keys = new_keys.at[:, 0].set(qkv[:, 1])
    new_values = new_values.at[:, 0].set(qkv[:, 2])
    keys = jnp.concatenate([cache_keys, new_keys], axis=1).reshape(own, count, heads_here, DH)
    values = jnp.concatenate([cache_values, new_values], axis=1).reshape(own, count, heads_here, DH)
    valid = jnp.broadcast_to(jnp.arange(count) < prev + 1, (own, count))
    mixed = attend(qkv[:, 0].reshape(own, heads_here, DH), keys, values, valid)
    resid = resid + from_owner(mixed.reshape(own, half_inner), w_self_out)
    normed = rms_norm(resid, norm_cross, width)
    query = to_owner(normed, w_cross_q).astype(jnp.bfloat16)
    mixed = attend(query.reshape(own, heads_here, DH), src_keys, src_values, valid_rows)
    resid = resid + from_owner(mixed.reshape(own, half_inner), w_cross_out)
    normed = rms_norm(resid, norm_ffn, width)
    gated = to_owner(normed, w_in).reshape(own, 2, -1)
    hidden = (jax.nn.gelu(gated[:, 0], approximate=True) * gated[:, 1]).astype(jnp.bfloat16)
    resid = resid + from_owner(hidden, w_out)
    outputs = [resid.astype(jnp.bfloat16)]
    stacked = jnp.stack(outputs)
    return stacked[:, slot_of]


def solution(mesh):
    in_specs = (
        P(),
        P(),
        P(),
        P(),
        P(None, None, "dev", "section"),
        P(None, "dev", None, "section"),
        P(None, "dev"),
        P("dev"),
        P("dev"),
        P("dev"),
        P("dev", None, "section"),
        P("section", "dev"),
        P("dev", "section"),
        P("section", "dev"),
        P("dev", None, "section"),
        P("section", "dev"),
    )
    out_specs = P(None, None, "dev")
    return jax.shard_map(local, mesh=mesh, in_specs=in_specs, out_specs=out_specs, check_vma=False)
```

profile of v0, /device:TPU:0, one launch (start us, length us, event | category | flops | bytes accessed | tf_op | source)
XLA Modules:
  0.0 641.5 jit_solution(2823838541899439890)
XLA Ops:
  6.5 2.0 sort.17
  10.0 5.0 gather_fusion.4
  15.0 8.5 %all-to-all-start = ((bf16[2,128,8,1024]{3,2,0,1:T(8,128)(2,1)}), bf16[2,128,8,1024]{3,2,0,1:T(8,128)(2,1)}, u32[]{:S(2)}, u32[]{:S(2)}) async-start(bf16[2,128,8,1024]{3,2,0,1:T(8,128)(2,1)} %bitcast.101), calls=%async_computation | async-start | bytes 8388608 | tf_op jit(solution)/shard_map/all_to_all | solution.py:84
  26.0 8.4 %gather_fusion.1 = bf16[16,256]{1,0:T(8,128)(2,1)S(1)} fusion(bf16[32128,256]{1,0:T(8,128)(2,1)} %param.26, s32[1024]{0:T(1024)S(1)} %pad_clamp_fusion.2), kind=kCustom, calls=%fused_computation.1 | custom fusion | bytes 16448 | tf_op jit(solution)/shard_map/gather | solution.py:94
  34.5 95.5 %psum.42 = f32[16]{0:T(128)S(1)} all-reduce(f32[16]{0:T(128)S(1)} %fusion.28), channel_id=1, replica_groups=mesh['section'=2,'dev'=16] {'dev'}, use_global_device_ids=true, to_apply=%region_2.3 | all-reduce | flops 16 | bytes 128 | tf_op jit(solution)/shard_map/psum | solution.py:15
  131.1 86.1 %all-reduce.7 = bf16[16,3072]{1,0:T(8,128)(2,1)S(1)} all-reduce(f32[16,3072]{1,0:T(8,128)S(1)} %fusion.50), channel_id=2, replica_groups=mesh['section'=2,'dev'=16] {'dev'}, use_global_device_ids=true, to_apply=%region_3.4.clone | all-reduce | flops 49152 | bytes 294912
  221.2 35.8 %all-gather = bf16[16,1,1024]{2,1,0:T(2,128)(2,1)S(1)} all-gather(bf16[1,1,1024]{2,1,0:T(2,128)(2,1)S(1)} %reshape.396), channel_id=1, replica_groups=mesh['section'=2,'dev'=16] {'dev'}, dimensions={0}, use_global_device_ids=true | all-gather | bytes 34816 | tf_op jit(solution)/shard_map/all_gather | solution.py:32
  258.3 3.4 psum.43
  261.7 38.6 %psum.44 = f32[16]{0:T(128)S(1)} all-reduce(f32[16]{0:T(128)S(1)} %multiply_reduce_fusion.1), channel_id=1, replica_groups=mesh['section'=2,'dev'=16] {'dev'}, use_global_device_ids=true, to_apply=%region_8.9 | all-reduce | flops 16 | bytes 128 | tf_op jit(solution)/shard_map/psum | solution.py:15
  301.6 72.0 %all-reduce.1 = bf16[16,1024]{1,0:T(8,128)(2,1)S(1)} all-reduce(f32[16,1024]{1,0:T(8,128)S(1)} %fusion.48), channel_id=3, replica_groups=mesh['section'=2,'dev'=16] {'dev'}, use_global_device_ids=true, to_apply=%region_9.10.clone | all-reduce | flops 16384 | bytes 98304
  375.0 3.7 copy.59
  379.8 2.6 copy.97
  382.4 1.8 fusion.65
  384.2 6.4 reshape.333
  390.6 4.4 fusion.2
  395.3 4.0 reshape.334
  399.3 4.5 fusion
  403.9 35.8 %all-gather.1 = bf16[16,1,1024]{2,1,0:T(2,128)(2,1)S(1)} all-gather(bf16[1,1,1024]{2,1,0:T(2,128)(2,1)S(1)} %reshape.398), channel_id=1, replica_groups=mesh['section'=2,'dev'=16] {'dev'}, dimensions={0}, use_global_device_ids=true | all-gather | bytes 34816 | tf_op jit(solution)/shard_map/all_gather | solution.py:32
  439.9 3.4 psum.45
  443.4 38.6 %psum.46 = f32[16]{0:T(128)S(1)} all-reduce(f32[16]{0:T(128)S(1)} %get-tuple-element.34), channel_id=1, replica_groups=mesh['section'=2,'dev'=16] {'dev'}, use_global_device_ids=true, to_apply=%region_14.15 | all-reduce | flops 16 | bytes 128 | tf_op jit(solution)/shard_map/psum | solution.py:15
  481.9 3.0 fusion.49
  484.9 103.5 %all-reduce.6.cloned.1.call-done = f32[16,5120]{1,0:T(8,128)} async-done(((f32[16,5120]{1,0:T(8,128)}), f32[16,5120]{1,0:T(8,128)}) %all-reduce.6.cloned.1.call-update) | async-done | bytes 327696
  590.2 39.6 %all-gather.2 = bf16[16,1,2560]{2,1,0:T(2,128)(2,1)S(1)} all-gather(bf16[1,1,2560]{2,1,0:T(2,128)(2,1)S(1)} %convert_bitcast_fusion), channel_id=1, replica_groups=mesh['section'=2,'dev'=16] {'dev'}, dimensions={0}, use_global_device_ids=true | all-gather | bytes 87040 | tf_op jit(solution)/shard_map/all_gather | solution.py:32
  630.1 3.4 psum.47
  (77 shorter events, 18.3 us)
Async XLA Ops:
  6.5 623.3 %copy-start = (bf16[2560,256]{1,0:T(8,128)(2,1)S(1)}, bf16[2560,256]{1,0:T(8,128)(2,1)}, u32[]{:S(2)}) copy-start(bf16[2560,256]{1,0:T(8,128)(2,1)} %param.35) | copy-start | bytes 3932164
  15.0 8.6 %copy-start.1 = (s32[1,16]{1,0:T(1,128)S(1)}, s32[1,16]{1,0:T(1,128)}, u32[]{:S(2)}) copy-start(s32[1,16]{1,0:T(1,128)} %param.20) | copy-start | bytes 196
  15.0 115.0 %copy-start.4 = (f32[256]{0:T(256)S(1)}, f32[256]{0:T(256)}, u32[]{:S(2)}) copy-start(f32[256]{0:T(256)} %param.27) | copy-start | bytes 3076
  15.0 364.8 %all-to-all-start = ((bf16[2,128,8,1024]{3,2,0,1:T(8,128)(2,1)}), bf16[2,128,8,1024]{3,2,0,1:T(8,128)(2,1)}, u32[]{:S(2)}, u32[]{:S(2)}) async-start(bf16[2,128,8,1024]{3,2,0,1:T(8,128)(2,1)} %bitcast.101), calls=%async_computation | async-start | bytes 8388608 | tf_op jit(solution)/shard_map/all_to_all | solution.py:84
  23.5 107.0 %copy-start.8 = (u32[32]{0:T(128)S(1)}, u32[32]{0:T(128)}, u32[]{:S(2)}) copy-start(u32[32]{0:T(128)} %constant.83) | copy-start | bytes 388
  23.5 565.0 %all-reduce.6.cloned.1.call-start = ((), (), s32[]{:S(2)}) async-start(), calls=%async_computation.1 | async-start | bytes 655360
  25.9 274.4 %copy-start.5 = (f32[256]{0:T(256)S(1)}, f32[256]{0:T(256)}, u32[]{:S(2)}) copy-start(f32[256]{0:T(256)} %param.28) | copy-start | bytes 3076
  25.9 348.4 %copy-start.2 = (s32[16]{0:T(128)S(1)}, s32[16]{0:T(128)}, u32[]{:S(2)}) copy-start(s32[16]{0:T(128)} %param.22) | copy-start | bytes 196
  395.3 86.7 %copy-start.6 = (f32[256]{0:T(256)S(1)}, f32[256]{0:T(256)}, u32[]{:S(2)}) copy-start(f32[256]{0:T(256)} %param.29) | copy-start | bytes 3076
  399.3 40.4 %copy-start.3 = (bf16[1024,256]{1,0:T(8,128)(2,1)S(1)}, bf16[1024,256]{1,0:T(8,128)(2,1)}, u32[]{:S(2)}) copy-start(bf16[1024,256]{1,0:T(8,128)(2,1)} %param.33) | copy-start | bytes 1572868
  399.3 85.6 %copy-start.7 = (s32[16]{0:T(128)S(1)}, s32[16]{0:T(128)}, u32[]{:S(2)}) copy-start(s32[16]{0:T(128)} %param.21) | copy-start | bytes 196
Sparse Core Ops, SparseCore 0:
  485.0 103.4 all-reduce.5
where the time goes:
time: 642 us; the launch traced here: 641 us
  blocking collectives  452 us (70%)
  waiting for transfers between devices  104 us (16%)
  local copies, waits for them, and re-layouts  44.3 us (7%)
  matrix products  15.6 us (2%)
  between operations  13.6 us (2%)
  starting transfers between devices  8.54 us (1%)
    psum x3, blocking collectives, rms_norm(): total = lax.psum(jnp.sum(resid * resid, axis=1), 'dev')  173 us
    unnamed x2, blocking collectives  158 us
    all_gather x3, blocking collectives, from_owner(): lax.all_gather(active, 'dev', axis=0, tiled=True)  111 us
    unnamed x2, waiting for transfers between devices  104 us
  transfers between devices with their start and end apart: 2, of which 1 were waited for; matrix products, arithmetic and copies ran while one was open for 4% of the time, Pallas kernels for 0%

commit v1 on v0

v1 whole, which is shorter than its diff:
```python
import jax
import jax.numpy as jnp
from jax import lax
from jax.sharding import PartitionSpec as P

DH = 64
EPS = 1e-06
LANES = 128


def project(resid, gain, weight):
    width = resid.shape[1] * lax.axis_size("dev")
    scaled = (resid * gain[None, :]).astype(jnp.bfloat16)
    part = jnp.dot(scaled, weight, preferred_element_type=jnp.float32)
    squares = jnp.sum(resid * resid, axis=1, keepdims=True)
    packed = jnp.concatenate([part, jnp.broadcast_to(squares, (resid.shape[0], LANES))], axis=1)
    total = lax.psum(packed, "dev")
    scale = lax.rsqrt(total[:, -1:] / width + EPS)
    return total[:, :-LANES] * scale


def output(active, weight):
    return lax.psum(jnp.dot(active, weight, preferred_element_type=jnp.float32), "section")


def own_rows(array, own):
    return lax.dynamic_slice_in_dim(array, lax.axis_index("dev") * own, own, 0)


def self_attend(query, key, value, cache):
    own, features = query.shape
    heads = features // DH
    pick = (jnp.arange(features)[:, None] // DH == jnp.arange(heads)[None, :])
    spread = jnp.where(pick[None], query[:, :, None], 0).astype(jnp.bfloat16)
    scores = jnp.einsum("rjf,rfh->rjh", cache[0], spread, preferred_element_type=jnp.float32)
    fresh = jnp.sum(
        (query.astype(jnp.float32) * key.astype(jnp.float32)).reshape(own, heads, DH), axis=2
    )
    top = jnp.maximum(jnp.max(scores, axis=1), fresh)
    weights = jnp.exp(scores - top[:, None, :])
    weight = jnp.exp(fresh - top)
    total = jnp.sum(weights, axis=1) + weight
    mixed = jnp.einsum(
        "rjh,rjf->rhf", weights.astype(jnp.bfloat16), cache[1], preferred_element_type=jnp.float32
    )
    mixed = jnp.sum(jnp.where(pick.T[None], mixed, 0.0), axis=1)
    wide = jnp.repeat(weight.astype(jnp.bfloat16).astype(jnp.float32), DH, axis=1)
    mixed = mixed + wide * value.astype(jnp.float32)
    return (mixed / jnp.repeat(total, DH, axis=1)).astype(jnp.bfloat16)


def cross_attend(query, pool, owner, valid):
    requests, features = query.shape
    heads = features // DH
    pick = (jnp.arange(features)[:, None] // DH == jnp.arange(heads)[None, :])
    spread = jnp.where(pick.T[None], query[:, None, :], 0).reshape(requests * heads, features)
    scores = lax.dot_general(
        spread, pool[0], (((1,), (1,)), ((), ())), preferred_element_type=jnp.float32
    )
    column = jnp.arange(requests * heads) // heads
    mask = (column[:, None] == owner[None, :]) & valid[None, :]
    top = lax.pmax(jnp.max(jnp.where(mask, scores, -jnp.inf), axis=1), "dev")[:, None]
    weights = jnp.where(mask, jnp.exp(jnp.where(mask, scores, top) - top), 0.0)
    total = jnp.sum(weights, axis=1).reshape(requests, heads)
    mixed = jnp.dot(weights.astype(jnp.bfloat16), pool[1], preferred_element_type=jnp.float32)
    mixed = jnp.sum(
        jnp.where(pick.T[None], mixed.reshape(requests, heads, features), 0.0), axis=1
    )
    packed = jnp.concatenate([mixed, jnp.pad(total, ((0, 0), (0, -heads % LANES)))], axis=1)
    packed = lax.psum(packed, "dev")
    total = packed[:, features : features + heads]
    return (packed[:, :features] / jnp.repeat(total, DH, axis=1)).astype(jnp.bfloat16)


def local(
    token_ids,
    slot_of,
    lengths,
    block_table,
    kv_pool,
    self_cache,
    embedding,
    norm_self,
    norm_cross,
    norm_ffn,
    w_self_qkv,
    w_self_out,
    w_cross_q,
    w_cross_out,
    w_in,
    w_out,
):
    dev_count = lax.axis_size("dev")
    requests, max_blocks = block_table.shape
    own = requests // dev_count
    half_inner = w_cross_q.shape[1]
    here = lax.axis_index("dev")
    blocks, rows_here = kv_pool.shape[1:3]
    block_rows = rows_here * dev_count

    slot_hot = slot_of[:, None] == jnp.arange(requests)[None, :]
    ids_slot = jnp.sum(jnp.where(slot_hot, token_ids[0][:, None], 0), axis=0)

    place = slot_of[:, None] * max_blocks + jnp.arange(max_blocks)[None, :] + 1
    hit = block_table.reshape(-1)[:, None] == jnp.arange(blocks)[None, :]
    holder = jnp.sum(jnp.where(hit, place.reshape(-1)[:, None], 0), axis=0) - 1
    span = jnp.sum(jnp.where(hit, jnp.repeat(lengths, max_blocks)[:, None], 0), axis=0)
    first = (holder % max_blocks) * block_rows + here * rows_here
    valid = (first[:, None] + jnp.arange(rows_here)[None, :] < span[:, None]).reshape(-1)
    owner = jnp.repeat(jnp.where(holder >= 0, holder // max_blocks, -1), rows_here)
    pool = kv_pool.reshape(2, blocks * rows_here, half_inner)

    resid = embedding[ids_slot].astype(jnp.float32)
    qkv = project(resid, norm_self, w_self_qkv.reshape(w_self_qkv.shape[0], -1))
    qkv = own_rows(qkv, own).astype(jnp.bfloat16).reshape(own, 3, half_inner)
    mixed = self_attend(qkv[:, 0], qkv[:, 1], qkv[:, 2], self_cache)
    mixed = lax.all_gather(mixed, "dev", axis=0, tiled=True)
    resid = resid + output(mixed, w_self_out)

    query = project(resid, norm_cross, w_cross_q).astype(jnp.bfloat16)
    mixed = cross_attend(query, pool, owner, valid)
    resid = resid + output(mixed, w_cross_out)

    gated = own_rows(project(resid, norm_ffn, w_in.reshape(w_in.shape[0], -1)), own)
    gated = gated.reshape(own, 2, -1)
    hidden = (jax.nn.gelu(gated[:, 0], approximate=True) * gated[:, 1]).astype(jnp.bfloat16)
    hidden = lax.all_gather(hidden, "dev", axis=0, tiled=True)
    resid = resid + output(hidden, w_out)
    out = jnp.dot(
        slot_hot.astype(jnp.bfloat16), resid.astype(jnp.bfloat16), preferred_element_type=jnp.float32
    )
    return out.astype(jnp.bfloat16)[None]


def solution(mesh):
    in_specs = (
        P(),
        P(),
        P(),
        P(),
        P(None, None, "dev", "section"),
        P(None, "dev", None, "section"),
        P(None, "dev"),
        P("dev"),
        P("dev"),
        P("dev"),
        P("dev", None, "section"),
        P("section", "dev"),
        P("dev", "section"),
        P("section", "dev"),
        P("dev", None, "section"),
        P("section", "dev"),
    )
    out_specs = P(None, None, "dev")
    return jax.shard_map(local, mesh=mesh, in_specs=in_specs, out_specs=out_specs, check_vma=False)
```

time: 642 us -> 598 us (0.931)
  blocking collectives: 452 us -> 131 us
  waiting for transfers between devices: 104 us -> 410 us
  local copies, waits for them, and re-layouts: 44.3 us -> 19.2 us
  starting transfers between devices: 8.54 us -> 0.13 us
  other arithmetic: 3.82 us -> 10.3 us
    psum x0 -> x4, waiting for transfers between devices: none -> 410 us  [the longest x3 314 us: project(): total = lax.psum(packed, 'dev')]
    psum x6 -> x3, blocking collectives: 183 us -> 10.1 us  [output(): lax.psum(jnp.dot(active, weight, preferred_element_type=jnp.float32), 'se...]
    unnamed x2 -> x0, blocking collectives: 158 us -> none
    unnamed x2 -> x4, waiting for transfers between devices: 104 us -> 0.07 us
    pmax x0 -> x1, blocking collectives: none -> 40.7 us  [cross_attend(): lax.pmax(jnp.max(jnp.where(mask, scores, -jnp.inf), axis=1), 'dev')[:, None]]
    all_gather x3 -> x2, blocking collectives: 111 us -> 80 us  [the longest x1 40.2 us: local(): hidden = lax.all_gather(hidden, 'dev', axis=0, tiled=True)]
    another operation x4 -> x0, local copies, waits for them, and re-layouts: 10.5 us -> none
    all_to_all x1 -> x0, starting transfers between devices: 8.5 us -> none  [local(): lax.all_to_all(picked, 'dev', split_axis=1, concat_axis=2, tiled=True)]
  transfers between devices with their start and end apart: 2 -> 4, of which waited for: 1 -> 4; matrix products, arithmetic and copies ran while one was open for 4% -> 1% of each run, Pallas kernels for 0% -> 0%
where the time goes in v1:
time: 598 us; the launch traced here: 597 us
  waiting for transfers between devices  410 us (69%)
  blocking collectives  131 us (22%)
  local copies, waits for them, and re-layouts  19.2 us (3%)
  matrix products  13.5 us (2%)
  between operations  13.4 us (2%)
  other arithmetic  10.3 us (2%)
    psum x3, waiting for transfers between devices, project(): total = lax.psum(packed, 'dev')  314 us
    psum x1, waiting for transfers between devices, cross_attend(): packed = lax.psum(packed, 'dev')  95.4 us
    pmax x1, blocking collectives, cross_attend(): lax.pmax(jnp.max(jnp.where(mask, scores, -jnp.inf), axis=1), 'dev')[:, None]  40.7 us
    all_gather x1, blocking collectives, local(): hidden = lax.all_gather(hidden, 'dev', axis=0, tiled=True)  40.2 us
    all_gather x1, blocking collectives, local(): mixed = lax.all_gather(mixed, 'dev', axis=0, tiled=True)  39.8 us
  transfers between devices with their start and end apart: 4, of which 4 were waited for; matrix products, arithmetic and copies ran while one was open for 1% of the time, Pallas kernels for 0%

profile of v1, /device:TPU:0, one launch (start us, length us, event | category | flops | bytes accessed | tf_op | source)
XLA Modules:
  0.0 597.0 jit_solution(15534350614748718236)
XLA Ops:
  7.5 1.7 copy.22
  9.2 8.4 %gather_fusion = bf16[16,256]{1,0:T(8,128)(2,1)S(1)} fusion(bf16[32128,256]{1,0:T(8,128)(2,1)} %param.22, s32[1024]{0:T(1024)S(1)} %pad_clamp_fusion), kind=kCustom, calls=%fused_computation | custom fusion | bytes 16448 | tf_op jit(solution)/shard_map/gather | solution.py:113
  20.2 107.7 %all-reduce.6.cloned.1.call-done = f32[16,3200]{1,0:T(8,128)} async-done(((f32[16,3200]{1,0:T(8,128)}), f32[16,3200]{1,0:T(8,128)}) %all-reduce.6.cloned.1.call-update) | async-done | bytes 204816 | tf_op jit(solution)/shard_map/psum | solution.py:17
  127.9 0.9 fusion.62
  129.4 0.9 slice.72
  131.2 1.2 fusion.87
  132.5 1.2 fusion.12
  134.2 39.8 %all-gather = bf16[16,1,1024]{2,1,0:T(2,128)(2,1)S(1)} all-gather(bf16[1,1,1024]{2,1,0:T(2,128)(2,1)S(1)} %convert_bitcast_fusion.1), channel_id=1, replica_groups=mesh['section'=2,'dev'=16] {'dev'}, dimensions={0}, use_global_device_ids=true | all-gather | bytes 34816 | tf_op jit(solution)/shard_map/all_gather | solution.py:117
  174.0 1.2 fusion.31
  175.2 3.4 psum.50
  179.7 99.5 %all-reduce.8.cloned.1.call-done = f32[16,1152]{1,0:T(8,128)} async-done(((f32[16,1152]{1,0:T(8,128)}), f32[16,1152]{1,0:T(8,128)}) %all-reduce.8.cloned.1.call-update) | async-done | bytes 73744 | tf_op jit(solution)/shard_map/psum | solution.py:17
  280.0 0.9 fusion.25
  281.0 2.5 select_reduce_fusion
  283.5 40.7 %pmax.7 = f32[256]{0:T(256)S(1)} all-reduce(f32[256]{0:T(256)S(1)} %get-tuple-element.17), channel_id=1, replica_groups=mesh['section'=2,'dev'=16] {'dev'}, use_global_device_ids=true, to_apply=%region_13.14 | all-reduce | flops 256 | bytes 2048 | tf_op jit(solution)/shard_map/pmax | solution.py:62
  324.7 2.4 fusion.9
  327.9 3.7 copy.26
  331.6 95.4 %all-reduce.10.cloned.1.call-done = f32[16,1152]{1,0:T(8,128)} async-done(((f32[16,1152]{1,0:T(8,128)}), f32[16,1152]{1,0:T(8,128)}) %all-reduce.10.cloned.1.call-update) | async-done | bytes 73744 | tf_op jit(solution)/shard_map/psum | solution.py:70
  427.9 1.0 fusion.29
  429.0 3.4 psum.53
  432.4 2.2 fusion.51
  435.5 107.0 %all-reduce.12.cloned.1.call-done = f32[16,5248]{1,0:T(8,128)} async-done(((f32[16,5248]{1,0:T(8,128)}), f32[16,5248]{1,0:T(8,128)}) %all-reduce.12.cloned.1.call-update) | async-done | bytes 335888 | tf_op jit(solution)/shard_map/psum | solution.py:17
  544.0 1.0 slice.81
  545.8 40.2 %all-gather.1 = bf16[16,1,2560]{2,1,0:T(2,128)(2,1)S(1)} all-gather(bf16[1,1,2560]{2,1,0:T(2,128)(2,1)S(1)} %convert_bitcast_fusion), channel_id=1, replica_groups=mesh['section'=2,'dev'=16] {'dev'}, dimensions={0}, use_global_device_ids=true | all-gather | bytes 87040 | tf_op jit(solution)/shard_map/all_gather | solution.py:127
  586.3 3.4 psum.55
  (86 shorter events, 14.0 us)
Async XLA Ops:
  6.5 579.5 %copy-start = (bf16[2560,256]{1,0:T(8,128)(2,1)S(1)}, bf16[2560,256]{1,0:T(8,128)(2,1)}, u32[]{:S(2)}) copy-start(bf16[2560,256]{1,0:T(8,128)(2,1)} %param.31) | copy-start | bytes 3932164
  6.5 11.1 %copy-start.4 = (f32[256]{0:T(256)S(1)}, f32[256]{0:T(256)}, u32[]{:S(2)}) copy-start(f32[256]{0:T(256)} %param.23) | copy-start | bytes 3076
  6.5 121.4 %all-reduce.6.cloned.1.call-start = ((), (), s32[]{:S(2)}) async-start(), calls=%async_computation | async-start | bytes 409600 | tf_op jit(solution)/shard_map/psum | solution.py:17
  7.4 11.7 %copy-start.8 = (s32[16]{0:T(128)S(1)}, s32[16]{0:T(128)}, u32[]{:S(2)}) copy-start(s32[16]{0:T(128)} %param.17) | copy-start | bytes 196
  7.4 11.8 %copy-start.7 = (s32[16]{0:T(128)S(1)}, s32[16]{0:T(128)}, u32[]{:S(2)}) copy-start(s32[16]{0:T(128)} %param.18) | copy-start | bytes 196
  7.5 12.0 %copy-start.3 = (s32[16,8]{0,1:T(8,128)S(1)}, s32[16,8]{0,1:T(8,128)}, u32[]{:S(2)}) copy-start(s32[16,8]{0,1:T(8,128)} %param.19) | copy-start | bytes 1540
  17.7 161.0 %copy-start.1 = (bf16[256,1024]{1,0:T(8,128)(2,1)S(1)}, bf16[256,1024]{1,0:T(8,128)(2,1)}, u32[]{:S(2)}) copy-start(bf16[256,1024]{1,0:T(8,128)(2,1)} %param.28) | copy-start | bytes 1572868
  17.7 161.0 %copy-start.5 = (f32[256]{0:T(256)S(1)}, f32[256]{0:T(256)}, u32[]{:S(2)}) copy-start(f32[256]{0:T(256)} %param.24) | copy-start | bytes 3076
  19.0 260.1 %all-reduce.8.cloned.1.call-start = ((), (), s32[]{:S(2)}) async-start(), calls=%async_computation.1 | async-start | bytes 147456 | tf_op jit(solution)/shard_map/psum | solution.py:17
  179.6 247.4 %all-reduce.10.cloned.1.call-start = ((), (), s32[]{:S(2)}) async-start(), calls=%async_computation.2 | async-start | bytes 147456 | tf_op jit(solution)/shard_map/psum | solution.py:70
  327.8 214.7 %all-reduce.12.cloned.1.call-start = ((), (), s32[]{:S(2)}) async-start(), calls=%async_computation.3 | async-start | bytes 671744 | tf_op jit(solution)/shard_map/psum | solution.py:17
  327.9 100.0 %copy-start.2 = (bf16[1024,256]{1,0:T(8,128)(2,1)S(1)}, bf16[1024,256]{1,0:T(8,128)(2,1)}, u32[]{:S(2)}) copy-start(bf16[1024,256]{1,0:T(8,128)(2,1)} %param.29) | copy-start | bytes 1572868
  327.9 104.5 %copy-start.6 = (f32[256]{0:T(256)S(1)}, f32[256]{0:T(256)}, u32[]{:S(2)}) copy-start(f32[256]{0:T(256)} %param.25) | copy-start | bytes 3076
Sparse Core Ops, SparseCore 0:
  19.1 108.7 all-reduce.5
  179.8 99.3 all-reduce.7
  328.0 99.0 all-reduce.9
  435.6 106.8 all-reduce.11

commit v2 on v1

--- a/solution.py
+++ b/solution.py
@@ -1,30 +1,149 @@
+import functools
+
 import jax
 import jax.numpy as jnp
 from jax import lax
+from jax.experimental import pallas as pl
+from jax.experimental.pallas import tpu as pltpu
 from jax.sharding import PartitionSpec as P
 
 DH = 64
 EPS = 1e-06
 LANES = 128
+LOWEST = -1e30
+
+
+def exchange_kernel(n, scatter, spread, combine, x_ref, out_ref, *scratch):
+    scratch = list(scratch)
+    me = lax.axis_index("dev")
+    section = lax.axis_index("section")
+
+    def peer(step):
+        return (section, lax.rem(me + step, n))
+
+    barrier = pltpu.get_barrier_semaphore()
+
+    @pl.loop(1, n)
+    def _(step):
+        pl.semaphore_signal(barrier, inc=1, device_id=peer(step), device_id_type=pl.DeviceIdType.MESH)
+
+    pl.semaphore_wait(barrier, n - 1)
+
+    if scatter:
+        held, sent, got = scratch[:3]
+        scratch = scratch[3:]
+
+        def chunk(step):
+            return pltpu.make_async_remote_copy(
+                src_ref=x_ref.at[lax.rem(me + step, n)],
+                dst_ref=held.at[step],
+                send_sem=sent.at[step],
+                recv_sem=got.at[step],
+                device_id=peer(step),
+                device_id_type=pl.DeviceIdType.MESH,
+            )
+
+        @pl.loop(1, n)
+        def _(step):
+            chunk(step).start()
+
+        held[0] = x_ref[me]
+
+        @pl.loop(1, n)
+        def _(step):
+            chunk(step).wait()
+
+        result = combine(held)
+    else:
+        result = combine(x_ref)
+
+    if not spread:
+        out_ref[...] = result
+        return
+    mine, full, sent, got = scratch
+    mine[...] = result
+
+    def row(step):
+        return pltpu.make_async_remote_copy(
+            src_ref=mine,
+            dst_ref=full.at[me],
+            send_sem=sent.at[step],
+            recv_sem=got.at[step],
+            device_id=peer(step),
+            device_id_type=pl.DeviceIdType.MESH,
+        )
+
+    @pl.loop(1, n)
+    def _(step):
+        row(step).start()
+
+    full[me] = result
+
+    @pl.loop(1, n)
+    def _(step):
+        row(step).wait()
+
+    out_ref[...] = full[...]
+
+
+def exchange(x, columns, combine, collective_id, scatter=True, spread=True):
+    n = lax.axis_size("dev")
+    own = x.shape[0] // n if scatter else x.shape[0]
+    width = x.shape[1]
+    scratch = []
+    if scatter:
+        x = x.reshape(n, own, width)
+        scratch += [pltpu.VMEM((n, own, width), jnp.float32)] + [pltpu.SemaphoreType.DMA((n,))] * 2
+    if spread:
+        scratch += [pltpu.VMEM((own, columns), jnp.float32), pltpu.VMEM((n, own, columns), jnp.float32)]
+        scratch += [pltpu.SemaphoreType.DMA((n,))] * 2
+    result = pl.pallas_call(
+        functools.partial(exchange_kernel, n, scatter, spread, combine),
+        out_shape=jax.ShapeDtypeStruct((n, own, columns) if spread else (own, columns), jnp.float32),
+        in_specs=[pl.BlockSpec(memory_space=pltpu.VMEM)],
+        out_specs=pl.BlockSpec(memory_space=pltpu.VMEM),
+        scratch_shapes=scratch,
+        compiler_params=pltpu.CompilerParams(
+            collective_id=collective_id, has_side_effects=True, vmem_limit_bytes=48 * 1024 * 1024
+        ),
+    )(x)
+    return result.reshape(-1, columns)
+
+
+def scaled_sum(width, held):
+    total = jnp.sum(held[...], axis=0)
+    squares = jnp.max(total[:, -LANES:], axis=1, keepdims=True)
+    return total[:, :-LANES] * lax.rsqrt(squares / width + EPS)
+
+
+def gated_sum(width, held):
+    gated = scaled_sum(width, held)
+    units = gated.shape[1] // 2
+    gate = gated[:, :units]
+    bent = 0.7978845608028654 * (gate + 0.044715 * (gate * gate * gate))
+    return 0.5 * gate * (1.0 + jnp.tanh(bent)) * gated[:, units:]
+
+
+def merged(features, held):
+    parts = held[...]
+    mixed, top, total = (parts[:, :, i * features : (i + 1) * features] for i in range(3))
+    factor = jnp.exp(top - jnp.max(top, axis=0)[None])
+    return jnp.sum(factor * mixed, axis=0) / jnp.sum(factor * total, axis=0)
+
+
+def unchanged(ref):
+    return ref[...]
 
 
 def project(resid, gain, weight):
-    width = resid.shape[1] * lax.axis_size("dev")
     scaled = (resid * gain[None, :]).astype(jnp.bfloat16)
     part = jnp.dot(scaled, weight, preferred_element_type=jnp.float32)
     squares = jnp.sum(resid * resid, axis=1, keepdims=True)
-    packed = jnp.concatenate([part, jnp.broadcast_to(squares, (resid.shape[0], LANES))], axis=1)
-    total = lax.psum(packed, "dev")
-    scale = lax.rsqrt(total[:, -1:] / width + EPS)
-    return total[:, :-LANES] * scale
+    return jnp.concatenate([part, jnp.broadcast_to(squares, (resid.shape[0], LANES))], axis=1)
 
 
 def output(active, weight):
     return lax.psum(jnp.dot(active, weight, preferred_element_type=jnp.float32), "section")
-
-
-def own_rows(array, own):
-    return lax.dynamic_slice_in_dim(array, lax.axis_index("dev") * own, own, 0)
 
 
 def self_attend(query, key, value, cache):
@@ -59,17 +178,16 @@
     )
     column = jnp.arange(requests * heads) // heads
     mask = (column[:, None] == owner[None, :]) & valid[None, :]
-    top = lax.pmax(jnp.max(jnp.where(mask, scores, -jnp.inf), axis=1), "dev")[:, None]
+    top = jnp.max(jnp.where(mask, scores, LOWEST), axis=1, keepdims=True)
     weights = jnp.where(mask, jnp.exp(jnp.where(mask, scores, top) - top), 0.0)
     total = jnp.sum(weights, axis=1).reshape(requests, heads)
     mixed = jnp.dot(weights.astype(jnp.bfloat16), pool[1], preferred_element_type=jnp.float32)
     mixed = jnp.sum(
         jnp.where(pick.T[None], mixed.reshape(requests, heads, features), 0.0), axis=1
     )
-    packed = jnp.concatenate([mixed, jnp.pad(total, ((0, 0), (0, -heads % LANES)))], axis=1)
-    packed = lax.psum(packed, "dev")
-    total = packed[:, features : features + heads]
-    return (packed[:, :features] / jnp.repeat(total, DH, axis=1)).astype(jnp.bfloat16)
+    top = jnp.repeat(top.reshape(requests, heads), DH, axis=1)
+    packed = jnp.concatenate([mixed, top, jnp.repeat(total, DH, axis=1)], axis=1)
+    return exchange(packed, features, functools.partial(merged, features), 3).astype(jnp.bfloat16)
 
 
 def local(
@@ -111,21 +229,22 @@
     pool = kv_pool.reshape(2, blocks * rows_here, half_inner)
 
     resid = embedding[ids_slot].astype(jnp.float32)
+    width = resid.shape[1] * dev_count
+    summed = functools.partial(scaled_sum, width)
     qkv = project(resid, norm_self, w_self_qkv.reshape(w_self_qkv.shape[0], -1))
-    qkv = own_rows(qkv, own).astype(jnp.bfloat16).reshape(own, 3, half_inner)
-    mixed = self_attend(qkv[:, 0], qkv[:, 1], qkv[:, 2], self_cache)
-    mixed = lax.all_gather(mixed, "dev", axis=0, tiled=True)
+    qkv = exchange(qkv, 3 * half_inner, summed, 0, spread=False)
+    qkv = qkv.astype(jnp.bfloat16).reshape(own, 3, half_inner)
+    mixed = self_attend(qkv[:, 0], qkv[:, 1], qkv[:, 2], self_cache).astype(jnp.float32)
+    mixed = exchange(mixed, half_inner, unchanged, 1, scatter=False).astype(jnp.bfloat16)
     resid = resid + output(mixed, w_self_out)
 
-    query = project(resid, norm_cross, w_cross_q).astype(jnp.bfloat16)
-    mixed = cross_attend(query, pool, owner, valid)
+    query = exchange(project(resid, norm_cross, w_cross_q), half_inner, summed, 2)
+    mixed = cross_attend(query.astype(jnp.bfloat16), pool, owner, valid)
     resid = resid + output(mixed, w_cross_out)
 
-    gated = own_rows(project(resid, norm_ffn, w_in.reshape(w_in.shape[0], -1)), own)
-    gated = gated.reshape(own, 2, -1)
-    hidden = (jax.nn.gelu(gated[:, 0], approximate=True) * gated[:, 1]).astype(jnp.bfloat16)
-    hidden = lax.all_gather(hidden, "dev", axis=0, tiled=True)
-    resid = resid + output(hidden, w_out)
+    gated = project(resid, norm_ffn, w_in.reshape(w_in.shape[0], -1))
+    hidden = exchange(gated, w_in.shape[2], functools.partial(gated_sum, width), 4)
+    resid = resid + output(hidden.astype(jnp.bfloat16), w_out)
     out = jnp.dot(
         slot_hot.astype(jnp.bfloat16), resid.astype(jnp.bfloat16), preferred_element_type=jnp.float32
     )

time: 598 us -> 107 us (0.18)
  waiting for transfers between devices: 410 us -> 0 us
  blocking collectives: 131 us -> 10.1 us
  Pallas kernels: 0 us -> 67.8 us
  between operations: 13.4 us -> 0.43 us
  other arithmetic: 10.3 us -> 2.9 us
    psum x4 -> x0, waiting for transfers between devices: 410 us -> none  [the longest x3 314 us: project(): total = lax.psum(packed, 'dev')]
    all_gather x2 -> x0, blocking collectives: 80 us -> none  [the longest x1 40.2 us: local(): hidden = lax.all_gather(hidden, 'dev', axis=0, tiled=True)]
    pallas_call x0 -> x5, Pallas kernels: none -> 67.8 us  [exchange(): pl.pallas_call(functools.partial(exchange_kernel, n, scatter, spread, com...]
    pmax x1 -> x0, blocking collectives: 40.7 us -> none  [cross_attend(): lax.pmax(jnp.max(jnp.where(mask, scores, -jnp.inf), axis=1), 'dev')[:, None]]
  transfers between devices with their start and end apart: 4 -> 0, of which waited for: 4 -> 0; matrix products, arithmetic and copies ran while one was open for 1% -> 0% of each run, Pallas kernels for 0% -> 0%
where the time goes in v2:
time: 107 us
  Pallas kernels  67.8 us (63%)
  local copies, waits for them, and re-layouts  14.7 us (14%)
  matrix products  10.9 us (10%)
  blocking collectives  10.1 us (9%)
  other arithmetic  2.9 us (3%)
    pallas_call x5, Pallas kernels, exchange(): pl.pallas_call(functools.partial(exchange_kernel, n, scatter, spread, com...  67.8 us
    psum x3, blocking collectives, output(): lax.psum(jnp.dot(active, weight, preferred_element_type=jnp.float32), 'se...  10.1 us
    gather x1, local copies, waits for them, and re-layouts, local(): resid = embedding[ids_slot].astype(jnp.float32)  8.37 us
    unnamed x22, local copies, waits for them, and re-layouts  3.95 us
    dot_general x1, matrix products, cross_attend(): lax.dot_general(spread, pool[0], (((1,), (1,)), ((), ())), preferred_elem...  2.48 us
    dot_general x1, matrix products, cross_attend(): jnp.dot(weights.astype(jnp.bfloat16), pool[1], preferred_element_type=jnp...  2.41 us

profile of v2, /device:TPU:0, one launch (start us, length us, event | category | flops | bytes accessed | tf_op | source)
XLA Modules:
  0.0 106.8 jit_solution(16381634812737369588)
XLA Ops:
  0.0 0.9 select_reduce_fusion.3
  0.9 8.4 %gather_fusion = bf16[16,256]{1,0:T(8,128)(2,1)S(1)} fusion(bf16[32128,256]{1,0:T(8,128)(2,1)} %param.22, s32[1024]{0:T(1024)S(1)} %pad_clamp_fusion), kind=kCustom, calls=%fused_computation | custom fusion | bytes 16448 | tf_op jit(solution)/shard_map/gather | solution.py:231
  9.3 1.7 %copy.20 = bf16[256,3,1024]{0,2,1:T(8,128)(2,1)S(1)} copy(bf16[256,3,1024]{2,0,1:T(8,128)(2,1)} %param.26) | data formatting | bytes 3145728 | tf_op args[10]
  11.0 0.5 fusion.40
  12.0 10.9 %shard_map.154 = f32[1,3072]{1,0:T(1,128)S(1)} custom-call(f32[16,1,3200]{2,1,0:T(1,128)S(1)} %reshape.439.x_ref), custom_call_target="tpu_custom_call" | custom-call | tf_op jit(solution)/shard_map/pallas_call | solution.py:100
  22.9 1.2 %fusion.66 = (f32[16]{0:T(128)S(1)}, f32[16,128]{1,0:T(8,128)S(1)}) fusion(bf16[2,1,128,1024]{3,2,1,0:T(8,128)(2,1)} %param.21, s32[1024]{0:T(1024)S(1)} %add_select_fusion, bf16[1024]{0:T(1024)(128)(2,1)S(1)} %slice_reduce_fusion), kind=kOutput, calls=%fused_computation.112 | convolution fusion | flops 4229104 | bytes 276544 | tf_op jit(solution)/shard_map/rjf,rfh->rjh/dot_general | solution.py:154
  24.8 1.2 %fusion.12 = f32[1024]{0:T(1024)S(1)} fusion(bf16[2,1,128,1024]{3,2,1,0:T(8,128)(2,1)} %param.21, f32[16,128]{1,0:T(8,128)S(1)} %get-tuple-element.16, f32[16]{0:T(128)S(1)} %get-tuple-element.10, s32[1024]{0:T(1024)S(1)} %add_select_fusion), kind=kOutput, calls=%fused_computation.10 | convolution fusion | flops 4246528 | bytes 278592 | tf_op jit(solution)/shard_map/rjh,rjf->rhf/dot_general | solution.py:162
  26.1 9.1 %shard_map.155 = f32[16,1,1024]{2,1,0:T(1,128)S(1)} custom-call(f32[1,1024]{1,0:T(1,128)S(1)} %convert_convert_fusion.x_ref), custom_call_target="tpu_custom_call" | custom-call | tf_op jit(solution)/shard_map/pallas_call | solution.py:100
  35.3 1.2 %fusion.30 = f32[16,256]{1,0:T(8,128)S(1)} fusion(bf16[1024,256]{1,0:T(8,128)(2,1)} %param.27, bf16[16,1,1024]{2,1,0:T(2,128)(2,1)S(1)} %convert_element_type.142), kind=kOutput, calls=%fused_computation.43 | convolution fusion | flops 8388608 | bytes 573440 | tf_op jit(solution)/shard_map/dot_general | solution.py:146
  36.5 3.4 %psum.21 = f32[16,256]{1,0:T(8,128)S(1)} all-reduce(f32[16,256]{1,0:T(8,128)S(1)} %fusion.30), channel_id=1, replica_groups=mesh['section'=2,'dev'=16] {'section'}, use_global_device_ids=true, to_apply=%region_6.7 | all-reduce | flops 4096 | bytes 32768 | tf_op jit(solution)/shard_map/psum | solution.py:146
  39.9 0.2 fusion.38
  40.3 15.2 %shard_map.156 = f32[16,1,1024]{2,1,0:T(1,128)S(1)} custom-call(f32[16,1,1152]{2,1,0:T(1,128)S(1)} %reshape.443.x_ref), custom_call_target="tpu_custom_call" | custom-call | tf_op jit(solution)/shard_map/pallas_call | solution.py:100
  56.8 2.5 %select_reduce_fusion = (f32[256]{0:T(256)S(1)}, f32[256,1024]{1,0:T(8,128)S(1)}) fusion(s32[1024]{0:T(1024)S(1)} %eq.117, s32[256]{0:T(256)S(1)} %and_select_fusion.2, pred[1024]{0:T(1024)(128)(4,1)S(1)} %lt.35, bf16[256,1024]{1,0:T(8,128)(2,1)S(1)} %bitcast.77, bf16[2,128,8,1024]{3,2,1,0:T(8,128)(2,1)} %param.20), kind=kOutput, calls=%fused_computation.14 | convolution fusion | flops 537919232 | bytes 3677184 | tf_op jit(solution)/shard_map/dot_general | solution.py:176
  59.2 0.5 fusion.15
  60.1 2.4 %fusion.9 = f32[16,1024]{1,0:T(8,128)S(1)} fusion(bf16[16,16,1024]{2,1,0:T(8,128)(2,1)S(1)} %bitcast.76, bf16[2,128,8,1024]{3,2,1,0:T(8,128)(2,1)} %param.20, pred[16,1024]{1,0:T(8,128)(4,1)S(1)} %iota_compare_fusion.2), kind=kOutput, calls=%fused_computation.8 | convolution fusion | flops 537378816 | bytes 2703360 | tf_op jit(solution)/shard_map/dot_general | solution.py:184
  62.9 12.9 %shard_map.157 = f32[16,1,1024]{2,1,0:T(1,128)S(1)} custom-call(f32[16,1,3072]{2,1,0:T(1,128)S(1)} %reshape.447.x_ref), custom_call_target="tpu_custom_call" | custom-call | tf_op jit(solution)/shard_map/pallas_call | solution.py:100
  76.0 3.4 %psum.22 = f32[16,256]{1,0:T(8,128)S(1)} all-reduce(f32[16,256]{1,0:T(8,128)S(1)} %fusion.27), channel_id=1, replica_groups=mesh['section'=2,'dev'=16] {'section'}, use_global_device_ids=true, to_apply=%region_13.14 | all-reduce | flops 4096 | bytes 32768 | tf_op jit(solution)/shard_map/psum | solution.py:146
  79.5 2.1 %copy.26 = bf16[32,8,2,2560]{3,1,2,0:T(8,128)(2,1)S(1)} copy(bf16[32,8,2,2560]{3,2,1,0:T(2,128)(2,1)} %bitcast.75) | data formatting | bytes 5242880
  81.6 0.5 fusion.39
  82.2 0.2 reshape.449.x_ref
  82.5 19.8 %shard_map.158 = f32[16,1,2560]{2,1,0:T(1,128)S(1)} custom-call(f32[16,1,5248]{2,1,0:T(1,128)S(1)} %reshape.449.x_ref), custom_call_target="tpu_custom_call" | custom-call | tf_op jit(solution)/shard_map/pallas_call | solution.py:100
  102.4 0.3 fusion.21
  102.7 3.4 %psum.23 = f32[16,256]{1,0:T(8,128)S(1)} all-reduce(f32[16,256]{1,0:T(8,128)S(1)} %fusion.21), channel_id=1, replica_groups=mesh['section'=2,'dev'=16] {'section'}, use_global_device_ids=true, to_apply=%region_15.16 | all-reduce | flops 4096 | bytes 32768 | tf_op jit(solution)/shard_map/psum | solution.py:146
  106.0 0.8 fusion.13
  (76 shorter events, 3.9 us)
Async XLA Ops:
  0.0 102.4 %copy-start = (bf16[2560,256]{1,0:T(8,128)(2,1)S(1)}, bf16[2560,256]{1,0:T(8,128)(2,1)}, u32[]{:S(2)}) copy-start(bf16[2560,256]{1,0:T(8,128)(2,1)} %param.31) | copy-start | bytes 3932164
  0.0 11.0 %copy-start.4 = (f32[256]{0:T(256)S(1)}, f32[256]{0:T(256)}, u32[]{:S(2)}) copy-start(f32[256]{0:T(256)} %param.23) | copy-start | bytes 3076
  11.0 28.9 %copy-start.1 = (bf16[256,1024]{1,0:T(8,128)(2,1)S(1)}, bf16[256,1024]{1,0:T(8,128)(2,1)}, u32[]{:S(2)}) copy-start(bf16[256,1024]{1,0:T(8,128)(2,1)} %param.28) | copy-start | bytes 1572868
  11.0 28.9 %copy-start.5 = (f32[256]{0:T(256)S(1)}, f32[256]{0:T(256)}, u32[]{:S(2)}) copy-start(f32[256]{0:T(256)} %param.24) | copy-start | bytes 3076
  11.8 43.9 %copy-start.8 = (s32[16]{0:T(128)S(1)}, s32[16]{0:T(128)}, u32[]{:S(2)}) copy-start(s32[16]{0:T(128)} %param.17) | copy-start | bytes 196
  11.8 44.1 %copy-start.7 = (s32[16]{0:T(128)S(1)}, s32[16]{0:T(128)}, u32[]{:S(2)}) copy-start(s32[16]{0:T(128)} %param.18) | copy-start | bytes 196
  11.8 44.2 %copy-start.3 = (s32[16,8]{0,1:T(8,128)S(1)}, s32[16,8]{0,1:T(8,128)}, u32[]{:S(2)}) copy-start(s32[16,8]{0,1:T(8,128)} %param.19) | copy-start | bytes 1540
  60.1 15.8 %copy-start.2 = (bf16[1024,256]{1,0:T(8,128)(2,1)S(1)}, bf16[1024,256]{1,0:T(8,128)(2,1)}, u32[]{:S(2)}) copy-start(bf16[1024,256]{1,0:T(8,128)(2,1)} %param.29) | copy-start | bytes 1572868
  79.5 2.1 %copy-start.6 = (f32[256]{0:T(256)S(1)}, f32[256]{0:T(256)}, u32[]{:S(2)}) copy-start(f32[256]{0:T(256)} %param.25) | copy-start | bytes 3076

commit v3 on v2

--- a/solution.py
+++ b/solution.py
@@ -140,6 +140,44 @@
     part = jnp.dot(scaled, weight, preferred_element_type=jnp.float32)
     squares = jnp.sum(resid * resid, axis=1, keepdims=True)
     return jnp.concatenate([part, jnp.broadcast_to(squares, (resid.shape[0], LANES))], axis=1)
+
+
+def embed_kernel(window, ids_ref, table_ref, out_ref, held, sem):
+    requests = out_ref.shape[0]
+
+    def fetch(index):
+        first = pl.multiple_of(ids_ref[index] // window * window, window)
+        return pltpu.make_async_copy(
+            table_ref.at[pl.ds(first, window)], held.at[index], sem.at[index]
+        )
+
+    @pl.loop(0, requests)
+    def _(index):
+        fetch(index).start()
+
+    @pl.loop(0, requests)
+    def _(index):
+        fetch(index).wait()
+        rows = held[index].astype(jnp.float32)
+        here = lax.broadcasted_iota(jnp.int32, rows.shape, 0) == ids_ref[index] % window
+        out_ref[pl.ds(index, 1)] = jnp.sum(jnp.where(here, rows, 0.0), axis=0, keepdims=True)
+
+
+def embed(ids, table):
+    window = 16
+    requests, width = ids.shape[0], table.shape[1]
+    if table.shape[0] % window:
+        return table[ids].astype(jnp.float32)
+    return pl.pallas_call(
+        functools.partial(embed_kernel, window),
+        out_shape=jax.ShapeDtypeStruct((requests, width), jnp.float32),
+        in_specs=[pl.BlockSpec(memory_space=pltpu.SMEM), pl.BlockSpec(memory_space=pl.ANY)],
+        out_specs=pl.BlockSpec(memory_space=pltpu.VMEM),
+        scratch_shapes=[
+            pltpu.VMEM((requests, window, width), table.dtype),
+            pltpu.SemaphoreType.DMA((requests,)),
+        ],
+    )(ids, table)
 
 
 def output(active, weight):
@@ -228,7 +266,7 @@
     owner = jnp.repeat(jnp.where(holder >= 0, holder // max_blocks, -1), rows_here)
     pool = kv_pool.reshape(2, blocks * rows_here, half_inner)
 
-    resid = embedding[ids_slot].astype(jnp.float32)
+    resid = embed(ids_slot, embedding)
     width = resid.shape[1] * dev_count
     summed = functools.partial(scaled_sum, width)
     qkv = project(resid, norm_self, w_self_qkv.reshape(w_self_qkv.shape[0], -1))

time: 107 us -> 102 us (0.953)
  local copies, waits for them, and re-layouts: 14.7 us -> 6.31 us
  Pallas kernels: 67.8 us -> 70.2 us
    gather x1 -> x0, local copies, waits for them, and re-layouts: 8.37 us -> none  [local(): resid = embedding[ids_slot].astype(jnp.float32)]
    pallas_call x0 -> x1, Pallas kernels: none -> 2.39 us  [embed(): pl.pallas_call(functools.partial(embed_kernel, window), out_shape=jax.Sha...]
    unnamed x22 -> x24, local copies, waits for them, and re-layouts: 3.95 us -> 3.96 us
where the time goes in v3:
time: 102 us; the launch traced here: 101 us
  Pallas kernels  70.2 us (69%)
  matrix products  11 us (11%)
  blocking collectives  10.1 us (10%)
  local copies, waits for them, and re-layouts  6.31 us (6%)
  other arithmetic  3.38 us (3%)
    pallas_call x5, Pallas kernels, exchange(): pl.pallas_call(functools.partial(exchange_kernel, n, scatter, spread, com...  67.8 us
    psum x3, blocking collectives, output(): lax.psum(jnp.dot(active, weight, preferred_element_type=jnp.float32), 'se...  10.1 us
    unnamed x24, local copies, waits for them, and re-layouts  3.96 us
    dot_general x1, matrix products, cross_attend(): lax.dot_general(spread, pool[0], (((1,), (1,)), ((), ())), preferred_elem...  2.52 us
    dot_general x1, matrix products, cross_attend(): jnp.dot(weights.astype(jnp.bfloat16), pool[1], preferred_element_type=jnp...  2.42 us
    pallas_call x1, Pallas kernels, embed(): pl.pallas_call(functools.partial(embed_kernel, window), out_shape=jax.Sha...  2.39 us

profile of v3, /device:TPU:0, one launch (start us, length us, event | category | flops | bytes accessed | tf_op | source)
XLA Modules:
  0.0 101.4 jit_solution(3492340961400212039)
XLA Ops:
  0.0 1.4 %select_reduce_fusion.3.ids_ref = s32[16]{0:T(128)} fusion(s32[16]{0:T(128)} %bitcast.76, s32[16]{0:T(128)} %param.17), kind=kLoop, calls=%fused_computation.67 | loop fusion | flops 752 | bytes 192 | tf_op jit(solution)/shard_map/reduce_sum | solution.py:258
  1.4 2.4 %shard_map.154 = f32[16,256]{1,0:T(8,128)} custom-call(s32[16]{0:T(128)} %select_reduce_fusion.3.ids_ref, bf16[32128,256]{1,0:T(8,128)(2,1)} %table_ref.1), custom_call_target="tpu_custom_call" | custom-call | tf_op jit(solution)/shard_map/pallas_call | solution.py:171
  3.8 1.7 %copy.20 = bf16[256,3,1024]{0,2,1:T(8,128)(2,1)S(1)} copy(bf16[256,3,1024]{2,0,1:T(8,128)(2,1)} %param.26) | data formatting | bytes 3145728 | tf_op args[10]
  5.6 0.5 fusion.36
  6.5 10.9 %shard_map.155 = f32[1,3072]{1,0:T(1,128)S(1)} custom-call(f32[16,1,3200]{2,1,0:T(1,128)S(1)} %reshape.426.x_ref), custom_call_target="tpu_custom_call" | custom-call | tf_op jit(solution)/shard_map/pallas_call | solution.py:100
  17.5 1.2 %fusion.60 = (f32[16]{0:T(128)S(1)}, f32[16,128]{1,0:T(8,128)S(1)}) fusion(bf16[2,1,128,1024]{3,2,1,0:T(8,128)(2,1)} %param.21, s32[1024]{0:T(1024)S(1)} %add_select_fusion, bf16[1024]{0:T(1024)(128)(2,1)S(1)} %slice_reduce_fusion), kind=kOutput, calls=%fused_computation.104 | convolution fusion | flops 4229104 | bytes 276544 | tf_op jit(solution)/shard_map/rjf,rfh->rjh/dot_general | solution.py:192
  19.3 1.2 %fusion.12 = f32[1024]{0:T(1024)S(1)} fusion(bf16[2,1,128,1024]{3,2,1,0:T(8,128)(2,1)} %param.21, f32[16,128]{1,0:T(8,128)S(1)} %get-tuple-element.18, f32[16]{0:T(128)S(1)} %get-tuple-element.12, s32[1024]{0:T(1024)S(1)} %add_select_fusion), kind=kOutput, calls=%fused_computation.9 | convolution fusion | flops 4246528 | bytes 278592 | tf_op jit(solution)/shard_map/rjh,rjf->rhf/dot_general | solution.py:200
  20.7 9.1 %shard_map.156 = f32[16,1,1024]{2,1,0:T(1,128)S(1)} custom-call(f32[1,1024]{1,0:T(1,128)S(1)} %convert_convert_fusion.x_ref), custom_call_target="tpu_custom_call" | custom-call | tf_op jit(solution)/shard_map/pallas_call | solution.py:100
  29.8 1.2 %fusion.30 = f32[16,256]{1,0:T(8,128)S(1)} fusion(bf16[1024,256]{1,0:T(8,128)(2,1)} %param.27, bf16[16,1,1024]{2,1,0:T(2,128)(2,1)S(1)} %convert_element_type.138), kind=kOutput, calls=%fused_computation.42 | convolution fusion | flops 8388608 | bytes 573440 | tf_op jit(solution)/shard_map/dot_general | solution.py:184
  31.0 3.4 %psum.21 = f32[16,256]{1,0:T(8,128)S(1)} all-reduce(f32[16,256]{1,0:T(8,128)S(1)} %fusion.30), channel_id=1, replica_groups=mesh['section'=2,'dev'=16] {'section'}, use_global_device_ids=true, to_apply=%region_6.7 | all-reduce | flops 4096 | bytes 32768 | tf_op jit(solution)/shard_map/psum | solution.py:184
  34.5 0.2 fusion.37
  34.9 15.2 %shard_map.157 = f32[16,1,1024]{2,1,0:T(1,128)S(1)} custom-call(f32[16,1,1152]{2,1,0:T(1,128)S(1)} %reshape.430.x_ref), custom_call_target="tpu_custom_call" | custom-call | tf_op jit(solution)/shard_map/pallas_call | solution.py:100
  51.3 2.5 %select_reduce_fusion = (f32[256]{0:T(256)S(1)}, f32[256,1024]{1,0:T(8,128)S(1)}) fusion(s32[1024]{0:T(1024)S(1)} %eq.117, s32[256]{0:T(256)S(1)} %and_select_fusion.2, pred[1024]{0:T(1024)(128)(4,1)S(1)} %lt.24, bf16[256,1024]{1,0:T(8,128)(2,1)S(1)} %bitcast.73, bf16[2,128,8,1024]{3,2,1,0:T(8,128)(2,1)} %param.20), kind=kOutput, calls=%fused_computation.13 | convolution fusion | flops 537919232 | bytes 3677184 | tf_op jit(solution)/shard_map/dot_general | solution.py:214
  53.8 0.5 fusion.15
  54.6 2.4 %fusion.9 = f32[16,1024]{1,0:T(8,128)S(1)} fusion(bf16[16,16,1024]{2,1,0:T(8,128)(2,1)S(1)} %bitcast.72, bf16[2,128,8,1024]{3,2,1,0:T(8,128)(2,1)} %param.20, pred[16,1024]{1,0:T(8,128)(4,1)S(1)} %iota_compare_fusion.2), kind=kOutput, calls=%fused_computation.7 | convolution fusion | flops 537378816 | bytes 2703360 | tf_op jit(solution)/shard_map/dot_general | solution.py:222
  57.5 12.9 %shard_map.158 = f32[16,1,1024]{2,1,0:T(1,128)S(1)} custom-call(f32[16,1,3072]{2,1,0:T(1,128)S(1)} %reshape.434.x_ref), custom_call_target="tpu_custom_call" | custom-call | tf_op jit(solution)/shard_map/pallas_call | solution.py:100
  70.6 3.4 %psum.22 = f32[16,256]{1,0:T(8,128)S(1)} all-reduce(f32[16,256]{1,0:T(8,128)S(1)} %fusion.27), channel_id=1, replica_groups=mesh['section'=2,'dev'=16] {'section'}, use_global_device_ids=true, to_apply=%region_13.14 | all-reduce | flops 4096 | bytes 32768 | tf_op jit(solution)/shard_map/psum | solution.py:184
  74.1 2.1 %copy.26 = bf16[32,8,2,2560]{3,1,2,0:T(8,128)(2,1)S(1)} copy(bf16[32,8,2,2560]{3,2,1,0:T(2,128)(2,1)} %bitcast.71) | data formatting | bytes 5242880
  76.2 0.5 fusion.38
  76.8 0.2 reshape.436.x_ref
  77.0 19.8 %shard_map.159 = f32[16,1,2560]{2,1,0:T(1,128)S(1)} custom-call(f32[16,1,5248]{2,1,0:T(1,128)S(1)} %reshape.436.x_ref), custom_call_target="tpu_custom_call" | custom-call | tf_op jit(solution)/shard_map/pallas_call | solution.py:100
  96.9 0.3 fusion.21
  97.2 3.4 %psum.23 = f32[16,256]{1,0:T(8,128)S(1)} all-reduce(f32[16,256]{1,0:T(8,128)S(1)} %fusion.21), channel_id=1, replica_groups=mesh['section'=2,'dev'=16] {'section'}, use_global_device_ids=true, to_apply=%region_15.16 | all-reduce | flops 4096 | bytes 32768 | tf_op jit(solution)/shard_map/psum | solution.py:184
  100.6 0.8 fusion.13
  (76 shorter events, 3.9 us)
Async XLA Ops:
  0.0 96.9 %copy-start = (bf16[2560,256]{1,0:T(8,128)(2,1)S(1)}, bf16[2560,256]{1,0:T(8,128)(2,1)}, u32[]{:S(2)}) copy-start(bf16[2560,256]{1,0:T(8,128)(2,1)} %param.31) | copy-start | bytes 3932164
  3.8 1.7 %copy-start.3 = (f32[16,256]{1,0:T(8,128)S(1)}, f32[16,256]{1,0:T(8,128)}, u32[]{:S(2)}) copy-start(f32[16,256]{1,0:T(8,128)} %shard_map.154) | copy-start | bytes 49156
  3.8 1.7 %copy-start.5 = (f32[256]{0:T(256)S(1)}, f32[256]{0:T(256)}, u32[]{:S(2)}) copy-start(f32[256]{0:T(256)} %param.23) | copy-start | bytes 3076
  5.5 29.0 %copy-start.1 = (bf16[256,1024]{1,0:T(8,128)(2,1)S(1)}, bf16[256,1024]{1,0:T(8,128)(2,1)}, u32[]{:S(2)}) copy-start(bf16[256,1024]{1,0:T(8,128)(2,1)} %param.28) | copy-start | bytes 1572868
  5.5 29.0 %copy-start.6 = (f32[256]{0:T(256)S(1)}, f32[256]{0:T(256)}, u32[]{:S(2)}) copy-start(f32[256]{0:T(256)} %param.24) | copy-start | bytes 3076
  6.3 43.9 %copy-start.9 = (s32[16]{0:T(128)S(1)}, s32[16]{0:T(128)}, u32[]{:S(2)}) copy-start(s32[16]{0:T(128)} %param.17) | copy-start | bytes 196
  6.3 44.1 %copy-start.8 = (s32[16]{0:T(128)S(1)}, s32[16]{0:T(128)}, u32[]{:S(2)}) copy-start(s32[16]{0:T(128)} %param.18) | copy-start | bytes 196
  6.3 44.2 %copy-start.4 = (s32[16,8]{0,1:T(8,128)S(1)}, s32[16,8]{0,1:T(8,128)}, u32[]{:S(2)}) copy-start(s32[16,8]{0,1:T(8,128)} %param.19) | copy-start | bytes 1540
  54.6 15.8 %copy-start.2 = (bf16[1024,256]{1,0:T(8,128)(2,1)S(1)}, bf16[1024,256]{1,0:T(8,128)(2,1)}, u32[]{:S(2)}) copy-start(bf16[1024,256]{1,0:T(8,128)(2,1)} %param.29) | copy-start | bytes 1572868
  74.1 2.1 %copy-start.7 = (f32[256]{0:T(256)S(1)}, f32[256]{0:T(256)}, u32[]{:S(2)}) copy-start(f32[256]{0:T(256)} %param.25) | copy-start | bytes 3076

commit v4 on v3

--- a/solution.py
+++ b/solution.py
@@ -23,7 +23,7 @@
 
     barrier = pltpu.get_barrier_semaphore()
 
-    @pl.loop(1, n)
+    @pl.loop(1, n, unroll=n <= 16)
     def _(step):
         pl.semaphore_signal(barrier, inc=1, device_id=peer(step), device_id_type=pl.DeviceIdType.MESH)
 
@@ -43,13 +43,13 @@
                 device_id_type=pl.DeviceIdType.MESH,
             )
 
-        @pl.loop(1, n)
+        @pl.loop(1, n, unroll=n <= 16)
         def _(step):
             chunk(step).start()
 
         held[0] = x_ref[me]
 
-        @pl.loop(1, n)
+        @pl.loop(1, n, unroll=n <= 16)
         def _(step):
             chunk(step).wait()
 
@@ -73,13 +73,13 @@
             device_id_type=pl.DeviceIdType.MESH,
         )
 
-    @pl.loop(1, n)
+    @pl.loop(1, n, unroll=n <= 16)
     def _(step):
         row(step).start()
 
     full[me] = result
 
-    @pl.loop(1, n)
+    @pl.loop(1, n, unroll=n <= 16)
     def _(step):
         row(step).wait()
 

time: 102 us -> 102 us (level)
  no operation moved by 1% of the time
where the time goes in v4:
time: 102 us; the launch traced here: 101 us
  Pallas kernels  69.9 us (69%)
  matrix products  11 us (11%)
  blocking collectives  10.1 us (10%)
  local copies, waits for them, and re-layouts  6.31 us (6%)
  other arithmetic  3.38 us (3%)
    pallas_call x5, Pallas kernels, exchange(): pl.pallas_call(functools.partial(exchange_kernel, n, scatter, spread, com...  67.5 us
    psum x3, blocking collectives, output(): lax.psum(jnp.dot(active, weight, preferred_element_type=jnp.float32), 'se...  10.1 us
    unnamed x24, local copies, waits for them, and re-layouts  3.96 us
    dot_general x1, matrix products, cross_attend(): lax.dot_general(spread, pool[0], (((1,), (1,)), ((), ())), preferred_elem...  2.53 us
    dot_general x1, matrix products, cross_attend(): jnp.dot(weights.astype(jnp.bfloat16), pool[1], preferred_element_type=jnp...  2.42 us
    pallas_call x1, Pallas kernels, embed(): pl.pallas_call(functools.partial(embed_kernel, window), out_shape=jax.Sha...  2.39 us

profile of v4, /device:TPU:0, one launch (start us, length us, event | category | flops | bytes accessed | tf_op | source)
XLA Modules:
  0.0 101.1 jit_solution(13733836170595569403)
XLA Ops:
  0.0 1.4 %select_reduce_fusion.3.ids_ref = s32[16]{0:T(128)} fusion(s32[16]{0:T(128)} %bitcast.76, s32[16]{0:T(128)} %param.17), kind=kLoop, calls=%fused_computation.67 | loop fusion | flops 752 | bytes 192 | tf_op jit(solution)/shard_map/reduce_sum | solution.py:258
  1.4 2.4 %shard_map.154 = f32[16,256]{1,0:T(8,128)} custom-call(s32[16]{0:T(128)} %select_reduce_fusion.3.ids_ref, bf16[32128,256]{1,0:T(8,128)(2,1)} %table_ref.1), custom_call_target="tpu_custom_call" | custom-call | tf_op jit(solution)/shard_map/pallas_call | solution.py:171
  3.8 1.7 %copy.20 = bf16[256,3,1024]{0,2,1:T(8,128)(2,1)S(1)} copy(bf16[256,3,1024]{2,0,1:T(8,128)(2,1)} %param.26) | data formatting | bytes 3145728 | tf_op args[10]
  5.6 0.5 fusion.36
  6.5 10.8 %shard_map.155 = f32[1,3072]{1,0:T(1,128)S(1)} custom-call(f32[16,1,3200]{2,1,0:T(1,128)S(1)} %reshape.426.x_ref), custom_call_target="tpu_custom_call" | custom-call | tf_op jit(solution)/shard_map/pallas_call | solution.py:100
  17.4 1.2 %fusion.60 = (f32[16]{0:T(128)S(1)}, f32[16,128]{1,0:T(8,128)S(1)}) fusion(bf16[2,1,128,1024]{3,2,1,0:T(8,128)(2,1)} %param.21, s32[1024]{0:T(1024)S(1)} %add_select_fusion, bf16[1024]{0:T(1024)(128)(2,1)S(1)} %slice_reduce_fusion), kind=kOutput, calls=%fused_computation.104 | convolution fusion | flops 4229104 | bytes 276544 | tf_op jit(solution)/shard_map/rjf,rfh->rjh/dot_general | solution.py:192
  19.2 1.2 %fusion.12 = f32[1024]{0:T(1024)S(1)} fusion(bf16[2,1,128,1024]{3,2,1,0:T(8,128)(2,1)} %param.21, f32[16,128]{1,0:T(8,128)S(1)} %get-tuple-element.18, f32[16]{0:T(128)S(1)} %get-tuple-element.12, s32[1024]{0:T(1024)S(1)} %add_select_fusion), kind=kOutput, calls=%fused_computation.9 | convolution fusion | flops 4246528 | bytes 278592 | tf_op jit(solution)/shard_map/rjh,rjf->rhf/dot_general | solution.py:200
  20.6 9.1 %shard_map.156 = f32[16,1,1024]{2,1,0:T(1,128)S(1)} custom-call(f32[1,1024]{1,0:T(1,128)S(1)} %convert_convert_fusion.x_ref), custom_call_target="tpu_custom_call" | custom-call | tf_op jit(solution)/shard_map/pallas_call | solution.py:100
  29.8 1.2 %fusion.30 = f32[16,256]{1,0:T(8,128)S(1)} fusion(bf16[1024,256]{1,0:T(8,128)(2,1)} %param.27, bf16[16,1,1024]{2,1,0:T(2,128)(2,1)S(1)} %convert_element_type.138), kind=kOutput, calls=%fused_computation.42 | convolution fusion | flops 8388608 | bytes 573440 | tf_op jit(solution)/shard_map/dot_general | solution.py:184
  31.0 3.4 %psum.21 = f32[16,256]{1,0:T(8,128)S(1)} all-reduce(f32[16,256]{1,0:T(8,128)S(1)} %fusion.30), channel_id=1, replica_groups=mesh['section'=2,'dev'=16] {'section'}, use_global_device_ids=true, to_apply=%region_6.7 | all-reduce | flops 4096 | bytes 32768 | tf_op jit(solution)/shard_map/psum | solution.py:184
  34.5 0.2 fusion.37
  34.8 15.1 %shard_map.157 = f32[16,1,1024]{2,1,0:T(1,128)S(1)} custom-call(f32[16,1,1152]{2,1,0:T(1,128)S(1)} %reshape.430.x_ref), custom_call_target="tpu_custom_call" | custom-call | tf_op jit(solution)/shard_map/pallas_call | solution.py:100
  51.2 2.5 %select_reduce_fusion = (f32[256]{0:T(256)S(1)}, f32[256,1024]{1,0:T(8,128)S(1)}) fusion(s32[1024]{0:T(1024)S(1)} %eq.117, s32[256]{0:T(256)S(1)} %and_select_fusion.2, pred[1024]{0:T(1024)(128)(4,1)S(1)} %lt.24, bf16[256,1024]{1,0:T(8,128)(2,1)S(1)} %bitcast.73, bf16[2,128,8,1024]{3,2,1,0:T(8,128)(2,1)} %param.20), kind=kOutput, calls=%fused_computation.13 | convolution fusion | flops 537919232 | bytes 3677184 | tf_op jit(solution)/shard_map/dot_general | solution.py:214
  53.8 0.5 fusion.15
  54.6 2.4 %fusion.9 = f32[16,1024]{1,0:T(8,128)S(1)} fusion(bf16[16,16,1024]{2,1,0:T(8,128)(2,1)S(1)} %bitcast.72, bf16[2,128,8,1024]{3,2,1,0:T(8,128)(2,1)} %param.20, pred[16,1024]{1,0:T(8,128)(4,1)S(1)} %iota_compare_fusion.2), kind=kOutput, calls=%fused_computation.7 | convolution fusion | flops 537378816 | bytes 2703360 | tf_op jit(solution)/shard_map/dot_general | solution.py:222
  57.4 12.6 %shard_map.158 = f32[16,1,1024]{2,1,0:T(1,128)S(1)} custom-call(f32[16,1,3072]{2,1,0:T(1,128)S(1)} %reshape.434.x_ref), custom_call_target="tpu_custom_call" | custom-call | tf_op jit(solution)/shard_map/pallas_call | solution.py:100
  70.3 3.4 %psum.22 = f32[16,256]{1,0:T(8,128)S(1)} all-reduce(f32[16,256]{1,0:T(8,128)S(1)} %fusion.27), channel_id=1, replica_groups=mesh['section'=2,'dev'=16] {'section'}, use_global_device_ids=true, to_apply=%region_13.14 | all-reduce | flops 4096 | bytes 32768 | tf_op jit(solution)/shard_map/psum | solution.py:184
  73.8 2.1 %copy.26 = bf16[32,8,2,2560]{3,1,2,0:T(8,128)(2,1)S(1)} copy(bf16[32,8,2,2560]{3,2,1,0:T(2,128)(2,1)} %bitcast.71) | data formatting | bytes 5242880
  75.9 0.5 fusion.38
  76.5 0.2 reshape.436.x_ref
  76.7 19.8 %shard_map.159 = f32[16,1,2560]{2,1,0:T(1,128)S(1)} custom-call(f32[16,1,5248]{2,1,0:T(1,128)S(1)} %reshape.436.x_ref), custom_call_target="tpu_custom_call" | custom-call | tf_op jit(solution)/shard_map/pallas_call | solution.py:100
  96.7 0.3 fusion.21
  97.0 3.4 %psum.23 = f32[16,256]{1,0:T(8,128)S(1)} all-reduce(f32[16,256]{1,0:T(8,128)S(1)} %fusion.21), channel_id=1, replica_groups=mesh['section'=2,'dev'=16] {'section'}, use_global_device_ids=true, to_apply=%region_15.16 | all-reduce | flops 4096 | bytes 32768 | tf_op jit(solution)/shard_map/psum | solution.py:184
  100.3 0.8 fusion.13
  (76 shorter events, 3.9 us)
Async XLA Ops:
  0.0 96.7 %copy-start = (bf16[2560,256]{1,0:T(8,128)(2,1)S(1)}, bf16[2560,256]{1,0:T(8,128)(2,1)}, u32[]{:S(2)}) copy-start(bf16[2560,256]{1,0:T(8,128)(2,1)} %param.31) | copy-start | bytes 3932164
  3.8 1.7 %copy-start.3 = (f32[16,256]{1,0:T(8,128)S(1)}, f32[16,256]{1,0:T(8,128)}, u32[]{:S(2)}) copy-start(f32[16,256]{1,0:T(8,128)} %shard_map.154) | copy-start | bytes 49156
  3.8 1.7 %copy-start.5 = (f32[256]{0:T(256)S(1)}, f32[256]{0:T(256)}, u32[]{:S(2)}) copy-start(f32[256]{0:T(256)} %param.23) | copy-start | bytes 3076
  5.5 29.0 %copy-start.1 = (bf16[256,1024]{1,0:T(8,128)(2,1)S(1)}, bf16[256,1024]{1,0:T(8,128)(2,1)}, u32[]{:S(2)}) copy-start(bf16[256,1024]{1,0:T(8,128)(2,1)} %param.28) | copy-start | bytes 1572868
  5.5 28.9 %copy-start.6 = (f32[256]{0:T(256)S(1)}, f32[256]{0:T(256)}, u32[]{:S(2)}) copy-start(f32[256]{0:T(256)} %param.24) | copy-start | bytes 3076
  6.3 43.8 %copy-start.9 = (s32[16]{0:T(128)S(1)}, s32[16]{0:T(128)}, u32[]{:S(2)}) copy-start(s32[16]{0:T(128)} %param.17) | copy-start | bytes 196
  6.3 44.0 %copy-start.8 = (s32[16]{0:T(128)S(1)}, s32[16]{0:T(128)}, u32[]{:S(2)}) copy-start(s32[16]{0:T(128)} %param.18) | copy-start | bytes 196
  6.3 44.2 %copy-start.4 = (s32[16,8]{0,1:T(8,128)S(1)}, s32[16,8]{0,1:T(8,128)}, u32[]{:S(2)}) copy-start(s32[16,8]{0,1:T(8,128)} %param.19) | copy-start | bytes 1540
  54.6 15.5 %copy-start.2 = (bf16[1024,256]{1,0:T(8,128)(2,1)S(1)}, bf16[1024,256]{1,0:T(8,128)(2,1)}, u32[]{:S(2)}) copy-start(bf16[1024,256]{1,0:T(8,128)(2,1)} %param.29) | copy-start | bytes 1572868
  73.8 2.1 %copy-start.7 = (f32[256]{0:T(256)S(1)}, f32[256]{0:T(256)}, u32[]{:S(2)}) copy-start(f32[256]{0:T(256)} %param.25) | copy-start | bytes 3076

commit v5 on v3

--- a/solution.py
+++ b/solution.py
@@ -137,9 +137,10 @@
 
 def project(resid, gain, weight):
     scaled = (resid * gain[None, :]).astype(jnp.bfloat16)
-    part = jnp.dot(scaled, weight, preferred_element_type=jnp.float32)
+    slices = [weight] if weight.ndim == 2 else [weight[:, i] for i in range(weight.shape[1])]
+    parts = [jnp.dot(scaled, each, preferred_element_type=jnp.float32) for each in slices]
     squares = jnp.sum(resid * resid, axis=1, keepdims=True)
-    return jnp.concatenate([part, jnp.broadcast_to(squares, (resid.shape[0], LANES))], axis=1)
+    return jnp.concatenate([*parts, jnp.broadcast_to(squares, (resid.shape[0], LANES))], axis=1)
 
 
 def embed_kernel(window, ids_ref, table_ref, out_ref, held, sem):
@@ -269,7 +270,7 @@
     resid = embed(ids_slot, embedding)
     width = resid.shape[1] * dev_count
     summed = functools.partial(scaled_sum, width)
-    qkv = project(resid, norm_self, w_self_qkv.reshape(w_self_qkv.shape[0], -1))
+    qkv = project(resid, norm_self, w_self_qkv)
     qkv = exchange(qkv, 3 * half_inner, summed, 0, spread=False)
     qkv = qkv.astype(jnp.bfloat16).reshape(own, 3, half_inner)
     mixed = self_attend(qkv[:, 0], qkv[:, 1], qkv[:, 2], self_cache).astype(jnp.float32)
@@ -280,7 +281,7 @@
     mixed = cross_attend(query.astype(jnp.bfloat16), pool, owner, valid)
     resid = resid + output(mixed, w_cross_out)
 
-    gated = project(resid, norm_ffn, w_in.reshape(w_in.shape[0], -1))
+    gated = project(resid, norm_ffn, w_in)
     hidden = exchange(gated, w_in.shape[2], functools.partial(gated_sum, width), 4)
     resid = resid + output(hidden.astype(jnp.bfloat16), w_out)
     out = jnp.dot(

time: 102 us -> 106 us (1.039)
  local copies, waits for them, and re-layouts: 6.31 us -> 8.96 us
    slice x0 -> x1, local copies, waits for them, and re-layouts: none -> 6.48 us  [project(): weight[:, i]]
    unnamed x24, local copies, waits for them, and re-layouts: 3.96 us -> 0.14 us
where the time goes in v5:
time: 106 us; the launch traced here: 105 us
  Pallas kernels  70.3 us (66%)
  matrix products  11.1 us (10%)
  blocking collectives  10.1 us (10%)
  local copies, waits for them, and re-layouts  8.96 us (8%)
  other arithmetic  4.08 us (4%)
    pallas_call x5, Pallas kernels, exchange(): pl.pallas_call(functools.partial(exchange_kernel, n, scatter, spread, com...  67.8 us
    psum x3, blocking collectives, output(): lax.psum(jnp.dot(active, weight, preferred_element_type=jnp.float32), 'se...  10.1 us
    slice x1, local copies, waits for them, and re-layouts, project(): weight[:, i]  6.48 us
    pallas_call x1, Pallas kernels, embed(): pl.pallas_call(functools.partial(embed_kernel, window), out_shape=jax.Sha...  2.54 us
    dot_general x1, matrix products, cross_attend(): lax.dot_general(spread, pool[0], (((1,), (1,)), ((), ())), preferred_elem...  2.53 us
    dot_general x1, matrix products, cross_attend(): jnp.dot(weights.astype(jnp.bfloat16), pool[1], preferred_element_type=jnp...  2.42 us

profile of v5, /device:TPU:0, one launch (start us, length us, event | category | flops | bytes accessed | tf_op | source)
XLA Modules:
  0.0 105.0 jit_solution(7534748858777582605)
XLA Ops:
  0.0 1.4 %select_reduce_fusion.3.ids_ref = s32[16]{0:T(128)} fusion(s32[16]{0:T(128)} %bitcast.86, s32[16]{0:T(128)} %param.17), kind=kLoop, calls=%fused_computation.76 | loop fusion | flops 752 | bytes 192 | tf_op jit(solution)/shard_map/reduce_sum | solution.py:259
  1.4 2.5 %shard_map.154 = f32[16,256]{1,0:T(8,128)} custom-call(s32[16]{0:T(128)} %select_reduce_fusion.3.ids_ref, bf16[32128,256]{1,0:T(8,128)(2,1)} %table_ref.1), custom_call_target="tpu_custom_call" | custom-call | tf_op jit(solution)/shard_map/pallas_call | solution.py:172
  3.9 0.8 multiply_convert_fusion.2
  5.2 0.2 fusion.22
  5.6 10.9 %shard_map.155 = f32[1,3072]{1,0:T(1,128)S(1)} custom-call(f32[16,1,3200]{2,1,0:T(1,128)S(1)} %reshape.419.x_ref), custom_call_target="tpu_custom_call" | custom-call | tf_op jit(solution)/shard_map/pallas_call | solution.py:100
  16.6 1.2 %fusion.68 = (f32[16]{0:T(128)S(1)}, f32[16,128]{1,0:T(8,128)S(1)}) fusion(bf16[2,1,128,1024]{3,2,1,0:T(8,128)(2,1)} %param.21, s32[1024]{0:T(1024)S(1)} %add_select_fusion, bf16[1024]{0:T(1024)(128)(2,1)S(1)} %slice_reduce_fusion), kind=kOutput, calls=%fused_computation.114 | convolution fusion | flops 4229104 | bytes 276544 | tf_op jit(solution)/shard_map/rjf,rfh->rjh/dot_general | solution.py:193
  18.4 1.2 %fusion.14 = f32[1024]{0:T(1024)S(1)} fusion(bf16[2,1,128,1024]{3,2,1,0:T(8,128)(2,1)} %param.21, f32[16,128]{1,0:T(8,128)S(1)} %get-tuple-element.22, f32[16]{0:T(128)S(1)} %get-tuple-element.12, s32[1024]{0:T(1024)S(1)} %add_select_fusion), kind=kOutput, calls=%fused_computation.13 | convolution fusion | flops 4246528 | bytes 278592 | tf_op jit(solution)/shard_map/rjh,rjf->rhf/dot_general | solution.py:201
  19.8 9.1 %shard_map.156 = f32[16,1,1024]{2,1,0:T(1,128)S(1)} custom-call(f32[1,1024]{1,0:T(1,128)S(1)} %convert_convert_fusion.x_ref), custom_call_target="tpu_custom_call" | custom-call | tf_op jit(solution)/shard_map/pallas_call | solution.py:100
  29.0 1.2 %fusion.41 = f32[16,256]{1,0:T(8,128)S(1)} fusion(bf16[1024,256]{1,0:T(8,128)(2,1)} %param.27, bf16[16,1,1024]{2,1,0:T(2,128)(2,1)S(1)} %convert_element_type.138), kind=kOutput, calls=%fused_computation.55 | convolution fusion | flops 8388608 | bytes 573440 | tf_op jit(solution)/shard_map/dot_general | solution.py:185
  30.2 3.4 %psum.21 = f32[16,256]{1,0:T(8,128)S(1)} all-reduce(f32[16,256]{1,0:T(8,128)S(1)} %fusion.41), channel_id=1, replica_groups=mesh['section'=2,'dev'=16] {'section'}, use_global_device_ids=true, to_apply=%region_6.7 | all-reduce | flops 4096 | bytes 32768 | tf_op jit(solution)/shard_map/psum | solution.py:185
  34.0 15.2 %shard_map.157 = f32[16,1,1024]{2,1,0:T(1,128)S(1)} custom-call(f32[16,1,1152]{2,1,0:T(1,128)S(1)} %reshape.423.x_ref), custom_call_target="tpu_custom_call" | custom-call | tf_op jit(solution)/shard_map/pallas_call | solution.py:100
  50.4 2.5 %select_reduce_fusion = (f32[256]{0:T(256)S(1)}, f32[256,1024]{1,0:T(8,128)S(1)}) fusion(s32[1024]{0:T(1024)S(1)} %eq.117, s32[256]{0:T(256)S(1)} %and_select_fusion.2, pred[1024]{0:T(1024)(128)(4,1)S(1)} %lt.24, bf16[256,1024]{1,0:T(8,128)(2,1)S(1)} %bitcast.83, bf16[2,128,8,1024]{3,2,1,0:T(8,128)(2,1)} %param.20), kind=kOutput, calls=%fused_computation.17 | convolution fusion | flops 537919232 | bytes 3677184 | tf_op jit(solution)/shard_map/dot_general | solution.py:215
  53.0 0.5 fusion.17
  53.8 2.4 %fusion.11 = f32[16,1024]{1,0:T(8,128)S(1)} fusion(bf16[16,16,1024]{2,1,0:T(8,128)(2,1)S(1)} %bitcast.82, bf16[2,128,8,1024]{3,2,1,0:T(8,128)(2,1)} %param.20, pred[16,1024]{1,0:T(8,128)(4,1)S(1)} %iota_compare_fusion.2), kind=kOutput, calls=%fused_computation.11 | convolution fusion | flops 537378816 | bytes 2703360 | tf_op jit(solution)/shard_map/dot_general | solution.py:223
  56.6 12.9 %shard_map.158 = f32[16,1,1024]{2,1,0:T(1,128)S(1)} custom-call(f32[16,1,3072]{2,1,0:T(1,128)S(1)} %reshape.427.x_ref), custom_call_target="tpu_custom_call" | custom-call | tf_op jit(solution)/shard_map/pallas_call | solution.py:100
  69.8 3.4 %psum.22 = f32[16,256]{1,0:T(8,128)S(1)} all-reduce(f32[16,256]{1,0:T(8,128)S(1)} %fusion.38), channel_id=1, replica_groups=mesh['section'=2,'dev'=16] {'section'}, use_global_device_ids=true, to_apply=%region_13.14 | all-reduce | flops 4096 | bytes 32768 | tf_op jit(solution)/shard_map/psum | solution.py:185
  73.2 6.5 %fusion.67 = (bf16[256,1,2560]{2,1,0:T(2,128)(2,1)S(1)}, bf16[256,1,2560]{2,1,0:T(2,128)(2,1)S(1)}) fusion(bf16[256,2,2560]{2,1,0:T(2,128)(2,1)} %param.30), kind=kLoop, calls=%fused_computation.113 | loop fusion | bytes 5242880 | tf_op jit(solution)/shard_map/slice | solution.py:140
  79.7 0.3 fusion.10
  80.0 0.3 fusion.9
  80.4 0.2 reshape.428.x_ref
  80.7 19.8 %shard_map.159 = f32[16,1,2560]{2,1,0:T(1,128)S(1)} custom-call(f32[16,1,5248]{2,1,0:T(1,128)S(1)} %reshape.428.x_ref), custom_call_target="tpu_custom_call" | custom-call | tf_op jit(solution)/shard_map/pallas_call | solution.py:100
  100.6 0.3 fusion.32
  100.9 3.4 %psum.23 = f32[16,256]{1,0:T(8,128)S(1)} all-reduce(f32[16,256]{1,0:T(8,128)S(1)} %fusion.32), channel_id=1, replica_groups=mesh['section'=2,'dev'=16] {'section'}, use_global_device_ids=true, to_apply=%region_15.16 | all-reduce | flops 4096 | bytes 32768 | tf_op jit(solution)/shard_map/psum | solution.py:185
  104.2 0.8 fusion.15
  (80 shorter events, 4.3 us)
Async XLA Ops:
  0.0 100.6 %copy-start = (bf16[2560,256]{1,0:T(8,128)(2,1)S(1)}, bf16[2560,256]{1,0:T(8,128)(2,1)}, u32[]{:S(2)}) copy-start(bf16[2560,256]{1,0:T(8,128)(2,1)} %param.31) | copy-start | bytes 3932164
  1.4 2.5 %copy-start.8 = (f32[256]{0:T(256)S(1)}, f32[256]{0:T(256)}, u32[]{:S(2)}) copy-start(f32[256]{0:T(256)} %param.23) | copy-start | bytes 3076
  1.4 3.4 %copy-start.1 = (bf16[256,3,1024]{2,0,1:T(8,128)(2,1)S(1)}, bf16[256,3,1024]{2,0,1:T(8,128)(2,1)}, u32[]{:S(2)}) copy-start(bf16[256,3,1024]{2,0,1:T(8,128)(2,1)} %param.26) | copy-start | bytes 4718596
  4.8 28.8 %copy-start.4 = (f32[16,256]{1,0:T(8,128)S(1)}, f32[16,256]{1,0:T(8,128)}, u32[]{:S(2)}) copy-start(f32[16,256]{1,0:T(8,128)} %shard_map.154) | copy-start | bytes 49156
  5.0 28.7 %copy-start.2 = (bf16[256,1024]{1,0:T(8,128)(2,1)S(1)}, bf16[256,1024]{1,0:T(8,128)(2,1)}, u32[]{:S(2)}) copy-start(bf16[256,1024]{1,0:T(8,128)(2,1)} %param.28) | copy-start | bytes 1572868
  5.0 28.7 %copy-start.7 = (f32[256]{0:T(256)S(1)}, f32[256]{0:T(256)}, u32[]{:S(2)}) copy-start(f32[256]{0:T(256)} %param.24) | copy-start | bytes 3076
  5.4 43.9 %copy-start.10 = (s32[16]{0:T(128)S(1)}, s32[16]{0:T(128)}, u32[]{:S(2)}) copy-start(s32[16]{0:T(128)} %param.17) | copy-start | bytes 196
  5.5 44.1 %copy-start.9 = (s32[16]{0:T(128)S(1)}, s32[16]{0:T(128)}, u32[]{:S(2)}) copy-start(s32[16]{0:T(128)} %param.18) | copy-start | bytes 196
  5.5 44.2 %copy-start.6 = (s32[16,8]{0,1:T(8,128)S(1)}, s32[16,8]{0,1:T(8,128)}, u32[]{:S(2)}) copy-start(s32[16,8]{0,1:T(8,128)} %param.19) | copy-start | bytes 1540
  53.8 15.8 %copy-start.3 = (bf16[1024,256]{1,0:T(8,128)(2,1)S(1)}, bf16[1024,256]{1,0:T(8,128)(2,1)}, u32[]{:S(2)}) copy-start(bf16[1024,256]{1,0:T(8,128)(2,1)} %param.29) | copy-start | bytes 1572868
  73.2 6.5 %copy-start.5 = (f32[256]{0:T(256)S(1)}, f32[256]{0:T(256)}, u32[]{:S(2)}) copy-start(f32[256]{0:T(256)} %param.25) | copy-start | bytes 3076
